TPU v7x, 256 devices: a whole 4x4x8 slice. The times are simulated.
256 devices in a mesh: rows: 128 (over z, y, x), out: 2 (over core).
Axes of the slice: x: 4, y: 4, z: 8, core: 2. Of those that a mesh axis runs over, the one named last changes fastest.
Arguments:
- features: float32 [131072, 256], P('rows'), may hold values from -8 to 8
- targets: float32 [131072, 512], P('rows', 'out'), may hold values from -6 to 6
- nugget: float32 [131072], P('rows'), may hold values from 0.3 to 1.5
- pattern: int32 [128, 5], P('rows'), may hold values from 0 to 1, as said below
Outputs:
- solution: float32 [131072, 512], P('rows', 'out')
- residual: float32 [131072, 512], P('rows', 'out')
- image: float32 [131072, 512], P('rows', 'out')
Inputs may be any that keep to these rules, and one draw needn't show every extreme that they name: pattern[i, 2 + o] = 1 marks a stored tile of row block i and column block i + o. The pattern is symmetric (pattern[i, 2 + o] = pattern[i + o, 2 - o]), every entry of column 2 is 1, entries whose column block falls outside 0 to 127 are 0, some row block holds all 5 tiles, and row block 127 holds its tiles with the 2 row blocks below it.
All inputs are finite; a program needn't handle non-finite values.
Results may differ from a plain program's by a relative error of at most 0.013.
Values may be sent and summed in bfloat16 or wider, within the bound.
A program may use at most 64 MiB of HBM per device.

v0:
```python
import math

import jax
import jax.numpy as jnp
from jax import lax
from jax.sharding import PartitionSpec as P

ITERS = 2


def from_behind(array, axis, by):
    count = lax.axis_size(axis)
    pairs = [(i, i + by) for i in range(count) if 0 <= i + by < count]
    return lax.ppermute(array, axis, pairs)


def wendland(rows_a, rows_b):
    norms_a = jnp.sum(rows_a * rows_a, axis=1)
    norms_b = jnp.sum(rows_b * rows_b, axis=1)
    cross = jnp.dot(
        rows_a, rows_b.T, precision=lax.Precision.HIGHEST, preferred_element_type=jnp.float32
    )
    dist_sq = jnp.maximum(norms_a[:, None] + norms_b[None, :] - 2.0 * cross, 0.0)
    radius = 1.25 * math.sqrt(2.0 * rows_a.shape[1])
    ratio = jnp.sqrt(dist_sq) / radius
    falloff = jnp.maximum(1.0 - ratio, 0.0)
    return falloff**4 * (4.0 * ratio + 1.0)


def body(features, targets, nugget, pattern):
    reach_max = (pattern.shape[1] - 1) // 2
    tile_rows = features.shape[0]
    columns = targets.shape[1]
    offsets = list(range(-reach_max, reach_max + 1))
    tile_masks = pattern[0].astype(jnp.float32)
    feature_at = {0: features}
    for offset in offsets:
        if offset != 0:
            feature_at[offset] = from_behind(features.astype(jnp.bfloat16), "rows", -offset).astype(
                features.dtype
            )
    kernels = {}
    totals = jnp.zeros((tile_rows,), jnp.float32)
    for offset in offsets:
        kernel = tile_masks[reach_max + offset] * wendland(features, feature_at[offset])
        kernels[offset] = kernel.astype(jnp.bfloat16)
        totals = totals + jnp.sum(kernel, axis=1)

    def operate(field):
        field16 = field.astype(jnp.bfloat16)
        arrived = {0: field16}
        for offset in offsets:
            if offset != 0:
                arrived[offset] = from_behind(field16, "rows", -offset)
        summed = jnp.zeros((tile_rows, columns), jnp.float32)
        for offset in offsets:
            kernel16 = kernels[offset]
            block16 = arrived[offset]
            summed = summed + jnp.dot(kernel16, block16, preferred_element_type=jnp.float32)
        return nugget[:, None] * field + (totals[:, None] * field + summed) / tile_rows

    solution = jnp.zeros_like(targets)
    residual = targets
    image = operate(residual)
    image_step = jnp.zeros_like(targets)
    search_image = jnp.zeros_like(targets)
    direction = jnp.zeros_like(targets)
    norm_prev = jnp.ones((columns,), jnp.float32)
    step_prev = jnp.ones((columns,), jnp.float32)
    for step in range(ITERS):
        norm_sq, cross_term = lax.psum(
            (jnp.sum(residual * residual, axis=0), jnp.sum(image * residual, axis=0)), "rows"
        )
        product = operate(image)
        if step == 0:
            momentum = jnp.zeros((columns,), jnp.float32)
            step_len = norm_sq / cross_term
        else:
            momentum = norm_sq / norm_prev
            step_len = norm_sq / (cross_term - momentum * norm_sq / step_prev)
        image_step = product + momentum * image_step
        search_image = image + momentum * search_image
        direction = residual + momentum * direction
        solution = solution + step_len * direction
        residual = residual - step_len * search_image
        image = image - step_len * image_step
        norm_prev = norm_sq
        step_prev = step_len
    return (solution, residual, image)


def solution(mesh):
    return jax.shard_map(
        body,
        mesh=mesh,
        in_specs=(P("rows", None), P("rows", "out"), P("rows"), P("rows", None)),
        out_specs=(P("rows", "out"), P("rows", "out"), P("rows", "out")),
        check_vma=False,
    )
```

profile of v0, /device:TPU:0, one launch (start us, length us, event | category | flops | bytes accessed | tf_op | source)
XLA Modules:
  0.0 858.9 jit_solution(12126866314059870924)
XLA Ops:
  0.7 1.9 multiply_reduce_fusion.7
  2.6 1.3 collective-permute-start.3
  3.9 1.3 collective-permute-start.2
  5.2 4.6 collective-permute-start.1
  9.8 6.1 collective-permute-start
  15.8 0.1 convert_element_type.53
  15.9 1.3 collective-permute-start.7
  17.2 0.7 fusion.35
  17.9 7.1 fusion.38
  25.0 0.8 fusion.23
  25.8 0.5 copy-done.10
  26.3 0.0 collective-permute-done.3
  26.3 1.3 collective-permute-start.6
  27.6 0.2 multiply_reduce_fusion.3
  27.8 22.4 %collective-permute-done.2 = bf16[1024,256]{1,0:T(8,128)(2,1)S(1)} collective-permute-done((bf16[1024,256]{1,0:T(8,128)(2,1)S(1)}, bf16[1024,256]{1,0:T(8,128)(2,1)S(1)}, u32[]{:S(2)}, u32[]{:S(2)}) %collective-permute-start.2) | collective-permute-done | bytes 524320 | tf_op jit(solution)/shard_map/ppermute | solution.py:14
  50.2 1.5 collective-permute-start.5
  51.7 0.2 multiply_reduce_fusion.4
  51.9 0.0 collective-permute-done.1
  51.9 6.9 collective-permute-start.4
  58.9 0.2 multiply_reduce_fusion.5
  59.1 0.0 collective-permute-done
  59.1 0.2 multiply_reduce_fusion.6
  59.3 5.7 fusion.39
  65.0 5.7 fusion.40
  70.7 0.0 collective-permute-done.5
  70.7 0.8 fusion.29
  71.5 0.5 copy-done.12
  72.0 5.7 fusion.37
  77.7 5.9 fusion.36
  83.7 0.8 fusion.10
  84.4 0.6 copy-done.15
  85.0 0.0 copy-start.5
  85.0 0.8 fusion.5
  85.8 0.0 collective-permute-done.6
  85.8 2.3 multiply_reduce_fusion.2
  88.1 1.3 collective-permute-start.11
  89.4 1.3 collective-permute-start.10
  90.7 9.1 %collective-permute-start.9 = (bf16[1024,256]{1,0:T(8,128)(2,1)}, bf16[1024,256]{1,0:T(8,128)(2,1)}, u32[]{:S(2)}, u32[]{:S(2)}) collective-permute-start(bf16[1024,256]{1,0:T(8,128)(2,1)} %get-tuple-element.16), channel_id=1, source_target_pairs={{0,2},{2,4},{4,6},{6,8},{8,10},{10,12},{12,14},{14,16},{16,18},{18... | collective-permute-start | bytes 1572872 | tf_op jit(solution)/shard_map/ppermute | solution.py:14
  99.8 7.7 collective-permute-start.8
  107.6 369.9 %all-reduce.1 = (f32[256]{0:T(256)S(1)}, f32[256]{0:T(256)S(1)}) all-reduce(f32[256]{0:T(256)S(1)} %get-tuple-element.6, f32[256]{0:T(256)S(1)} %get-tuple-element.5), channel_id=1, replica_groups=mesh['rows'=128,'out'=2] {'rows'}, use_global_device_ids=true, to_apply=%region_1.0 | all-reduce | flops 512 | bytes 4096 | tf_op jit(solution)/shard_map/psum | solution.py:71
  477.5 2.6 fusion.21
  480.1 1.9 fusion.8
  482.0 1.8 fusion.27
  483.8 0.0 copy-start.2
  483.9 0.0 collective-permute-done.8
  483.9 2.0 fusion.3
  485.9 0.1 copy-done.8
  485.9 3.3 multiply_reduce_fusion
  489.2 342.3 %all-reduce = (f32[256]{0:T(256)S(1)}, f32[256]{0:T(256)S(1)}) all-reduce(f32[256]{0:T(256)S(1)} %get-tuple-element.4, f32[256]{0:T(256)S(1)} %get-tuple-element.3), channel_id=1, replica_groups=mesh['rows'=128,'out'=2] {'rows'}, use_global_device_ids=true, to_apply=%region_15.0 | all-reduce | flops 512 | bytes 4096 | tf_op jit(solution)/shard_map/psum | solution.py:71
  831.5 3.7 fusion.34
  835.2 1.4 collective-permute-start.15
  836.7 1.3 collective-permute-start.14
  838.0 4.6 collective-permute-start.13
  842.5 6.9 collective-permute-start.12
  849.4 0.7 fusion.19
  850.2 0.0 collective-permute-done.15
  850.2 0.8 fusion.6
  851.0 0.0 collective-permute-done.13
  851.0 0.8 copy-done.14
  851.8 0.7 fusion.25
  852.5 0.0 copy-start.3
  852.5 3.3 collective-permute-done.12
  855.8 0.8 fusion.1
  856.6 2.3 multiply_subtract_fusion
  (38 shorter events, 0.1 us)
Async XLA Ops:
  0.6 15.2 %copy-start = (f32[1024,256]{1,0:T(8,128)S(1)}, f32[1024,256]{1,0:T(8,128)}, u32[]{:S(2)}) copy-start(f32[1024,256]{1,0:T(8,128)} %param.5) | copy-start | bytes 3145732
  0.6 17.3 %copy-start.1 = (f32[1024,256]{1,0:T(8,128)S(1)}, f32[1024,256]{1,0:T(8,128)}, u32[]{:S(2)}) copy-start(f32[1024,256]{1,0:T(8,128)} %param.4) | copy-start | bytes 3145732
  0.7 16.5 %copy-start.6 = (s32[1,5]{1,0:T(1,128)S(1)}, s32[1,5]{1,0:T(1,128)}, u32[]{:S(2)}) copy-start(s32[1,5]{1,0:T(1,128)} %param.7) | copy-start | bytes 64
  2.6 23.8 %collective-permute-start.3 = (bf16[1024,256]{1,0:T(8,128)(2,1)S(1)}, bf16[1024,256]{1,0:T(8,128)(2,1)S(1)}, u32[]{:S(2)}, u32[]{:S(2)}) collective-permute-start(bf16[1024,256]{1,0:T(8,128)(2,1)S(1)} %get-tuple-element.18), channel_id=1, source_target_pairs={{4,0},{6,2},{8,4},{10,6},{12,8},{14,10},{16,12},{18,14},{20,16},{2... | collective-permute-start | bytes 1572872 | tf_op jit(solution)/shard_map/ppermute | solution.py:14
  3.9 46.3 %collective-permute-start.2 = (bf16[1024,256]{1,0:T(8,128)(2,1)S(1)}, bf16[1024,256]{1,0:T(8,128)(2,1)S(1)}, u32[]{:S(2)}, u32[]{:S(2)}) collective-permute-start(bf16[1024,256]{1,0:T(8,128)(2,1)S(1)} %get-tuple-element.18), channel_id=1, source_target_pairs={{2,0},{4,2},{6,4},{8,6},{10,8},{12,10},{14,12},{16,14},{18,16},{20... | collective-permute-start | bytes 1572872 | tf_op jit(solution)/shard_map/ppermute | solution.py:14
  5.2 46.7 %collective-permute-start.1 = (bf16[1024,256]{1,0:T(8,128)(2,1)S(1)}, bf16[1024,256]{1,0:T(8,128)(2,1)S(1)}, u32[]{:S(2)}, u32[]{:S(2)}) collective-permute-start(bf16[1024,256]{1,0:T(8,128)(2,1)S(1)} %get-tuple-element.18), channel_id=1, source_target_pairs={{0,2},{2,4},{4,6},{6,8},{8,10},{10,12},{12,14},{14,16},{16,18},{18... | collective-permute-start | bytes 1572872 | tf_op jit(solution)/shard_map/ppermute | solution.py:14
  9.8 49.3 %collective-permute-start = (bf16[1024,256]{1,0:T(8,128)(2,1)S(1)}, bf16[1024,256]{1,0:T(8,128)(2,1)S(1)}, u32[]{:S(2)}, u32[]{:S(2)}) collective-permute-start(bf16[1024,256]{1,0:T(8,128)(2,1)S(1)} %get-tuple-element.18), channel_id=1, source_target_pairs={{0,4},{2,6},{4,8},{6,10},{8,12},{10,14},{12,16},{14,18},{16,20},{1... | collective-permute-start | bytes 1572872 | tf_op jit(solution)/shard_map/ppermute | solution.py:14
  15.9 67.8 %collective-permute-start.7 = (bf16[1024,256]{1,0:T(8,128)(2,1)S(1)}, bf16[1024,256]{1,0:T(8,128)(2,1)S(1)}, u32[]{:S(2)}, u32[]{:S(2)}) collective-permute-start(bf16[1024,256]{1,0:T(8,128)(2,1)S(1)} %convert_element_type.53), channel_id=1, source_target_pairs={{4,0},{6,2},{8,4},{10,6},{12,8},{14,10},{16,12},{18,14},{20,16},{2... | collective-permute-start | bytes 1572872 | tf_op jit(solution)/shard_map/ppermute | solution.py:14
  25.0 1.3 copy-start.10
  26.3 59.5 %collective-permute-start.6 = (bf16[1024,256]{1,0:T(8,128)(2,1)S(1)}, bf16[1024,256]{1,0:T(8,128)(2,1)S(1)}, u32[]{:S(2)}, u32[]{:S(2)}) collective-permute-start(bf16[1024,256]{1,0:T(8,128)(2,1)S(1)} %convert_element_type.53), channel_id=1, source_target_pairs={{2,0},{4,2},{6,4},{8,6},{10,8},{12,10},{14,12},{16,14},{18,16},{20... | collective-permute-start | bytes 1572872 | tf_op jit(solution)/shard_map/ppermute | solution.py:14
  50.2 20.5 %collective-permute-start.5 = (bf16[1024,256]{1,0:T(8,128)(2,1)S(1)}, bf16[1024,256]{1,0:T(8,128)(2,1)S(1)}, u32[]{:S(2)}, u32[]{:S(2)}) collective-permute-start(bf16[1024,256]{1,0:T(8,128)(2,1)S(1)} %convert_element_type.53), channel_id=1, source_target_pairs={{0,2},{2,4},{4,6},{6,8},{8,10},{10,12},{12,14},{14,16},{16,18},{18... | collective-permute-start | bytes 1572872 | tf_op jit(solution)/shard_map/ppermute | solution.py:14
  51.9 33.1 %collective-permute-start.4 = (bf16[1024,256]{1,0:T(8,128)(2,1)S(1)}, bf16[1024,256]{1,0:T(8,128)(2,1)S(1)}, u32[]{:S(2)}, u32[]{:S(2)}) collective-permute-start(bf16[1024,256]{1,0:T(8,128)(2,1)S(1)} %convert_element_type.53), channel_id=1, source_target_pairs={{0,4},{2,6},{4,8},{6,10},{8,12},{10,14},{12,16},{14,18},{16,20},{1... | collective-permute-start | bytes 1572872 | tf_op jit(solution)/shard_map/ppermute | solution.py:14
  70.7 1.3 copy-start.12
  77.7 8.1 copy-start.7
  83.6 1.3 copy-start.15
  85.0 0.8 copy-start.5
  88.1 392.0 %collective-permute-start.11 = (bf16[1024,256]{1,0:T(8,128)(2,1)}, bf16[1024,256]{1,0:T(8,128)(2,1)}, u32[]{:S(2)}, u32[]{:S(2)}) collective-permute-start(bf16[1024,256]{1,0:T(8,128)(2,1)} %get-tuple-element.16), channel_id=1, source_target_pairs={{4,0},{6,2},{8,4},{10,6},{12,8},{14,10},{16,12},{18,14},{20,16},{2... | collective-permute-start | bytes 1572872 | tf_op jit(solution)/shard_map/ppermute | solution.py:14
  89.4 396.5 %collective-permute-start.10 = (bf16[1024,256]{1,0:T(8,128)(2,1)}, bf16[1024,256]{1,0:T(8,128)(2,1)}, u32[]{:S(2)}, u32[]{:S(2)}) collective-permute-start(bf16[1024,256]{1,0:T(8,128)(2,1)} %get-tuple-element.16), channel_id=1, source_target_pairs={{2,0},{4,2},{6,4},{8,6},{10,8},{12,10},{14,12},{16,14},{18,16},{20... | collective-permute-start | bytes 1572872 | tf_op jit(solution)/shard_map/ppermute | solution.py:14
  90.7 391.3 %collective-permute-start.9 = (bf16[1024,256]{1,0:T(8,128)(2,1)}, bf16[1024,256]{1,0:T(8,128)(2,1)}, u32[]{:S(2)}, u32[]{:S(2)}) collective-permute-start(bf16[1024,256]{1,0:T(8,128)(2,1)} %get-tuple-element.16), channel_id=1, source_target_pairs={{0,2},{2,4},{4,6},{6,8},{8,10},{10,12},{12,14},{14,16},{16,18},{18... | collective-permute-start | bytes 1572872 | tf_op jit(solution)/shard_map/ppermute | solution.py:14
  99.8 384.0 %collective-permute-start.8 = (bf16[1024,256]{1,0:T(8,128)(2,1)}, bf16[1024,256]{1,0:T(8,128)(2,1)}, u32[]{:S(2)}, u32[]{:S(2)}) collective-permute-start(bf16[1024,256]{1,0:T(8,128)(2,1)} %get-tuple-element.16), channel_id=1, source_target_pairs={{0,4},{2,6},{4,8},{6,10},{8,12},{10,14},{12,16},{14,18},{16,20},{1... | collective-permute-start | bytes 1572872 | tf_op jit(solution)/shard_map/ppermute | solution.py:14
  477.5 2.6 copy-start.16
  480.1 2.0 copy-start.13
  483.8 2.0 copy-start.2
  483.8 2.1 copy-start.8
  831.5 17.9 %copy-start.11 = (bf16[1024,1024]{0,1:T(8,128)(2,1)S(1)}, bf16[1024,1024]{0,1:T(8,128)(2,1)}, u32[]{:S(2)}) copy-start(bf16[1024,1024]{0,1:T(8,128)(2,1)} %copy-done.10) | copy-start | bytes 6291460
  835.2 15.0 %copy-start.17 = (bf16[1024,1024]{0,1:T(8,128)(2,1)S(1)}, bf16[1024,1024]{0,1:T(8,128)(2,1)}, u32[]{:S(2)}) copy-start(bf16[1024,1024]{0,1:T(8,128)(2,1)} %copy-done.15) | copy-start | bytes 6291460
  835.2 15.0 %collective-permute-start.15 = (bf16[1024,256]{1,0:T(8,128)(2,1)S(1)}, bf16[1024,256]{1,0:T(8,128)(2,1)S(1)}, u32[]{:S(2)}, u32[]{:S(2)}) collective-permute-start(bf16[1024,256]{1,0:T(8,128)(2,1)S(1)} %get-tuple-element.13), channel_id=1, source_target_pairs={{4,0},{6,2},{8,4},{10,6},{12,8},{14,10},{16,12},{18,14},{20,16},{2... | collective-permute-start | bytes 1572872 | tf_op jit(solution)/shard_map/ppermute | solution.py:14
  836.7 19.9 %collective-permute-start.14 = (bf16[1024,256]{1,0:T(8,128)(2,1)S(1)}, bf16[1024,256]{1,0:T(8,128)(2,1)S(1)}, u32[]{:S(2)}, u32[]{:S(2)}) collective-permute-start(bf16[1024,256]{1,0:T(8,128)(2,1)S(1)} %get-tuple-element.13), channel_id=1, source_target_pairs={{2,0},{4,2},{6,4},{8,6},{10,8},{12,10},{14,12},{16,14},{18,16},{20... | collective-permute-start | bytes 1572872 | tf_op jit(solution)/shard_map/ppermute | solution.py:14
  838.0 13.0 %collective-permute-start.13 = (bf16[1024,256]{1,0:T(8,128)(2,1)S(1)}, bf16[1024,256]{1,0:T(8,128)(2,1)S(1)}, u32[]{:S(2)}, u32[]{:S(2)}) collective-permute-start(bf16[1024,256]{1,0:T(8,128)(2,1)S(1)} %get-tuple-element.13), channel_id=1, source_target_pairs={{0,2},{2,4},{4,6},{6,8},{8,10},{10,12},{12,14},{14,16},{16,18},{18... | collective-permute-start | bytes 1572872 | tf_op jit(solution)/shard_map/ppermute | solution.py:14
  842.5 13.3 %collective-permute-start.12 = (bf16[1024,256]{1,0:T(8,128)(2,1)S(1)}, bf16[1024,256]{1,0:T(8,128)(2,1)S(1)}, u32[]{:S(2)}, u32[]{:S(2)}) collective-permute-start(bf16[1024,256]{1,0:T(8,128)(2,1)S(1)} %get-tuple-element.13), channel_id=1, source_target_pairs={{0,4},{2,6},{4,8},{6,10},{8,12},{10,14},{12,16},{14,18},{16,20},{1... | collective-permute-start | bytes 1572872 | tf_op jit(solution)/shard_map/ppermute | solution.py:14
  850.2 1.6 copy-start.14
  852.5 4.1 copy-start.3
  852.5 4.1 copy-start.4
  852.5 4.1 copy-start.9
where the time goes:
time: 874 us; the launch traced here: 859 us
  blocking collectives  712 us (81%)
  starting transfers between devices  57.8 us (7%)
  matrix products  52.3 us (6%)
  waiting for transfers between devices  25.7 us (3%)
    psum x2, blocking collectives, body(): lax.psum((jnp.sum(residual * residual, axis=0), jnp.sum(image * residual,...  712 us
    ppermute x16, starting transfers between devices, from_behind(): return lax.ppermute(array, axis, pairs)  57.8 us
    dot_general x5, matrix products, wendland(): jnp.dot(rows_a, rows_b.T, precision=lax.Precision.HIGHEST, preferred_elem...  30.1 us
    ppermute x16, waiting for transfers between devices, from_behind(): return lax.ppermute(array, axis, pairs)  25.7 us
    dot_general x15, matrix products, operate(): jnp.dot(kernel16, block16, preferred_element_type=jnp.float32)  22.2 us
  transfers between devices with their start and end apart: 16, of which 2 were waited for; matrix products, arithmetic and copies ran while one was open for 5% of the time, Pallas kernels for 0%

commit v1 on v0

v1 whole, which is shorter than its diff:
```python
import functools
import math

import jax
import jax.numpy as jnp
from jax import lax
from jax.experimental import pallas as pl
from jax.experimental.pallas import tpu as pltpu
from jax.sharding import PartitionSpec as P

MESH = pl.DeviceIdType.MESH
F32, BF16 = jnp.float32, jnp.bfloat16
NT = (((1,), (1,)), ((), ()))
X, Y, Z = 4, 4, 8
NB = X * Y * Z
T = 1024
D = 256
G = 128
H = T // 2
RADIUS = 1.25 * math.sqrt(2.0 * D) / math.sqrt(2.0)
M2, M1, P1, P2 = range(4)
TILE_OF = (0, 1, 3, 4)
COPIES = (
    (None, 1, 1, M1),
    (None, 0, -1, P1),
    (None, 0, 1, M1),
    (None, 1, -1, P1),
    (M1, 1, 1, M2),
    (P1, 0, -1, P2),
    (P2, 0, Y, M2),
    (M2, 1, -Y, P2),
)


def kernel(
    f_hbm, t_hbm, n_ref, pat_ref, sol_hbm, res_hbm, img_hbm,
    f32, t32, f16, fn, na, ktile, diag, x16, nb, cur, w1s, w2s, r1s, obuf, coef, xb, yb, zb,
    in_sem, out_sem, f_send, f_recv, sib_send, sib_recv, e_send, e_recv, ar_send, ar_recv,
):
    r, c = lax.axis_index("rows"), lax.axis_index("out")
    x, y, z = lax.rem(r, X), lax.rem(r // X, Y), r // (X * Y)

    def at(step):
        return (lax.rem(r + step + NB, NB), c)

    def along(axis, d):
        if axis == 0:
            return ((z * Y + y) * X + lax.rem(x + d, X), c)
        if axis == 1:
            return ((z * Y + lax.rem(y + d, Y)) * X + x, c)
        return ((lax.rem(z + d, Z) * Y + y) * X + x, c)

    sibling = (r, 1 - c)
    load_f = pltpu.make_async_copy(f_hbm, f32, in_sem.at[0])
    load_t = pltpu.make_async_copy(t_hbm, t32, in_sem.at[1])
    load_f.start()
    load_t.start()

    barrier = pltpu.get_barrier_semaphore()
    peers = [at(1), at(-1), at(Y), at(-Y), sibling]
    for axis, size in enumerate((X, Y, Z)):
        peers += [along(axis, d) for d in range(1, size)]
    for peer in peers:
        pl.semaphore_signal(barrier, inc=1, device_id=peer, device_id_type=MESH)

    def feature_rows(half):
        return pl.ds(pl.multiple_of(c * H + half * (H // 2), H // 2), H // 2)

    def f_copy(i):
        src, half, to, dst = COPIES[i]
        rows = feature_rows(half)
        return pltpu.make_async_remote_copy(
            src_ref=f16.at[rows] if src is None else fn.at[src, rows],
            dst_ref=fn.at[dst, rows],
            send_sem=f_send.at[i], recv_sem=f_recv.at[i],
            device_id=at(to), device_id_type=MESH,
        )

    def s_copy(slot):
        rows = pl.ds(pl.multiple_of(c * H, H), H)
        return pltpu.make_async_remote_copy(
            src_ref=fn.at[slot, rows], dst_ref=fn.at[slot, rows],
            send_sem=sib_send.at[slot], recv_sem=sib_recv.at[slot],
            device_id=sibling, device_id_type=MESH,
        )

    def e_copy(s, i):
        src, half, to, dst = COPIES[i]
        rows = pl.ds(half * H, H)
        return pltpu.make_async_remote_copy(
            src_ref=x16.at[s, rows] if src is None else nb.at[s, src, rows],
            dst_ref=nb.at[s, dst, rows],
            send_sem=e_send.at[s, i], recv_sem=e_recv.at[s, i],
            device_id=at(to), device_id_type=MESH,
        )

    def ar_buf(axis, k):
        return ((xb, x), (yb, y), (zb, z))[axis]

    def ar_copies(k, axis):
        buf, own = ar_buf(axis, k)
        first = (0, X - 1, X + Y - 2)[axis]
        return [
            pltpu.make_async_remote_copy(
                src_ref=buf.at[k, own], dst_ref=buf.at[k, own],
                send_sem=ar_send.at[k, first + d - 1], recv_sem=ar_recv.at[k, first + d - 1],
                device_id=along(axis, d), device_id_type=MESH,
            )
            for d in range(1, (X, Y, Z)[axis])
        ]

    def ar_start(k, axis, value):
        buf, own = ar_buf(axis, k)
        buf[k, own] = value
        for copy in ar_copies(k, axis):
            copy.start()

    def ar_finish(k, axis):
        for copy in ar_copies(k, axis):
            copy.wait_recv()
        buf, _ = ar_buf(axis, k)
        total = buf[k, 0]
        for i in range(1, (X, Y, Z)[axis]):
            total = total + buf[k, i]
        return total

    load_f.wait()
    f16[...] = f32[...].astype(BF16)
    pl.semaphore_wait(barrier, len(peers))
    for i in range(4):
        f_copy(i).start()
    load_t.wait()
    for g in range(2):
        x16[g] = t32[:, g * G:(g + 1) * G].astype(BF16)
        cur[g] = t32[:, g * G:(g + 1) * G]
        for i in range(4):
            e_copy(g, i).start()

    def squares(block):
        wide = block.astype(F32)
        sq = wide * wide
        high = sq.astype(BF16)
        return high, (sq - high.astype(F32)).astype(BF16)

    halves_col = jnp.full((D, G), 0.5, BF16)
    halves_row = jnp.full((16, D), 0.5, BF16)
    high, low = squares(f16[...])
    na[...] = jnp.dot(high, halves_col, preferred_element_type=F32) + jnp.dot(
        low, halves_col, preferred_element_type=F32
    )
    diag[...] = jnp.zeros_like(diag)

    def build(tile, other):
        high, low = squares(other[...])
        norms = lax.dot_general(halves_row, high, NT, preferred_element_type=F32) + lax.dot_general(
            halves_row, low, NT, preferred_element_type=F32
        )
        kept = pat_ref[0, tile].astype(F32)
        base = kept * (1.0 / (RADIUS**4 * T))
        slope = kept * (4.0 / (RADIUS**5 * T))

        def chunk(i, _):
            rows = pl.ds(pl.multiple_of(i * H, H), H)
            cross = lax.dot_general(f16[rows, :], other[...], NT, preferred_element_type=F32)
            norm = na[rows, :]
            summed = diag[rows, :]
            for lane in range(T // G):
                cols = slice(lane * G, (lane + 1) * G)
                half_sq = jnp.maximum(norm + norms[0:1, cols] - cross[:, cols], 1e-30)
                dist = half_sq * lax.rsqrt(half_sq)
                fall = jnp.maximum(RADIUS - dist, 0.0)
                fall = fall * fall
                value = (fall * fall) * (dist * slope + base)
                ktile[tile, rows, cols] = value.astype(BF16)
                summed = summed + value
            diag[rows, :] = summed
            return 0

        lax.fori_loop(0, T // H, chunk, 0)

    build(2, f16)
    f_copy(0).wait_recv()
    f_copy(4).start()
    f_copy(1).wait_recv()
    f_copy(5).start()
    f_copy(2).wait_recv()
    s_copy(M1).start()
    f_copy(3).wait_recv()
    s_copy(P1).start()
    s_copy(M1).wait_recv()
    build(1, fn.at[M1])
    f_copy(4).wait_recv()
    f_copy(7).start()
    f_copy(5).wait_recv()
    f_copy(6).start()
    s_copy(P1).wait_recv()
    build(3, fn.at[P1])
    e_copy(0, 0).wait_recv()
    e_copy(0, 4).start()
    e_copy(0, 1).wait_recv()
    e_copy(0, 5).start()
    f_copy(6).wait_recv()
    s_copy(M2).start()
    f_copy(7).wait_recv()
    s_copy(P2).start()
    s_copy(M2).wait_recv()
    build(0, fn.at[M2])
    e_copy(0, 4).wait_recv()
    e_copy(0, 7).start()
    e_copy(0, 5).wait_recv()
    e_copy(0, 6).start()
    e_copy(1, 0).wait_recv()
    e_copy(1, 4).start()
    e_copy(1, 1).wait_recv()
    e_copy(1, 5).start()
    s_copy(P2).wait_recv()
    build(4, fn.at[P2])
    nugget = jnp.broadcast_to(n_ref[0:1, :], (G, T)).T
    diag[...] = nugget + jnp.sum(diag[...], axis=1, keepdims=True)

    def out_copy(g, i):
        cols = pl.ds(pl.multiple_of(g * G, G), G)
        out = (sol_hbm, res_hbm, img_hbm)[i]
        return pltpu.make_async_copy(obuf.at[g, i], out.at[:, cols], out_sem.at[g, i])

    def step(s, _):
        g, e = lax.rem(s, 2), s // 2
        cols = pl.ds(pl.multiple_of(g * G, G), G)

        @pl.when(s >= 1)
        def _():
            e_copy(s, 4).wait_recv()
            e_copy(s, 7).start()
            e_copy(s, 5).wait_recv()
            e_copy(s, 6).start()

        @pl.when((s >= 1) & (s <= 4))
        def _():
            ar_start(s - 1, 1, ar_finish(s - 1, 0))
            e_copy(s + 1, 0).wait_recv()
            e_copy(s + 1, 4).start()
            e_copy(s + 1, 1).wait_recv()
            e_copy(s + 1, 5).start()
            ar_start(s - 1, 2, ar_finish(s - 1, 1))

        @pl.when(e == 1)
        def _():
            total = ar_finish(s - 2, 2)
            norm, cross = total[0:1, :], total[1:2, :]
            coef[g, 0:1, :] = norm
            coef[g, 1:2, :] = norm / cross

        @pl.when(e == 2)
        def _():
            total = ar_finish(s - 2, 2)
            norm, cross = total[0:1, :], total[1:2, :]
            step0 = coef[g, 1:2, :]
            momentum = norm / coef[g, 0:1, :]
            step1 = norm / (cross - momentum * norm / step0)
            coef[g, 2:3, :] = momentum
            coef[g, 3:4, :] = step1
            start = t32[:, cols]
            res = r1s[g]
            obuf[g, 0] = step0 * start + step1 * (res + momentum * start)
            obuf[g, 1] = res - step1 * (cur[g] + momentum * w1s[g])
            out_copy(g, 0).start()
            out_copy(g, 1).start()

        for i in (2, 3, 6, 7):
            e_copy(s, i).wait_recv()

        def chunk(i, sums):
            rows = pl.ds(pl.multiple_of(i * H, H), H)
            acc = jnp.dot(ktile[2, rows, :], x16[s], preferred_element_type=F32)
            for slot in (M1, P1, M2, P2):
                acc = acc + jnp.dot(
                    ktile[TILE_OF[slot], rows, :], nb[s, slot], preferred_element_type=F32
                )
            w2s[g, rows] = acc + diag[rows, :] * cur[g, rows]
            return sums

        lax.fori_loop(0, 2, chunk, 0)

        def reduce_start(norm, cross):
            ar_start(s, 0, jnp.concatenate(
                [jnp.sum(norm, axis=0, keepdims=True), jnp.sum(cross, axis=0, keepdims=True),
                 jnp.zeros((6, G), F32)], axis=0))

        @pl.when(e == 0)
        def _():
            w = w2s[g]
            x16[s + 2] = w.astype(BF16)
            for i in range(4):
                e_copy(s + 2, i).start()
            start = t32[:, cols]
            cur[g] = w
            w1s[g] = w
            reduce_start(start * start, w * start)

        @pl.when(e == 1)
        def _():
            step0 = coef[g, 1:2, :]
            image = cur[g] - step0 * w2s[g]
            x16[s + 2] = image.astype(BF16)
            for i in range(4):
                e_copy(s + 2, i).start()
            cur[g] = image
            res = t32[:, cols] - step0 * w1s[g]
            r1s[g] = res
            obuf[g, 2] = w2s[g]
            reduce_start(res * res, image * res)

        @pl.when(e == 2)
        def _():
            momentum, step1 = coef[g, 2:3, :], coef[g, 3:4, :]
            obuf[g, 2] = cur[g] - step1 * (w2s[g] + momentum * obuf[g, 2])
            out_copy(g, 2).start()

        return 0

    lax.fori_loop(0, 6, step, 0)

    for i in range(8):
        f_copy(i).wait_send()
    for slot in range(4):
        s_copy(slot).wait_send()

    def drain(s, _):
        for i in range(8):
            e_copy(s, i).wait_send()

        @pl.when(s < 4)
        def _():
            for axis in range(3):
                for copy in ar_copies(s, axis):
                    copy.wait_send()

        @pl.when(s < 2)
        def _():
            for i in range(3):
                out_copy(s, i).wait()

        return 0

    lax.fori_loop(0, 6, drain, 0)


def body(features, targets, nugget, pattern):
    out = jax.ShapeDtypeStruct((T, 2 * G), F32)
    dma = pltpu.SemaphoreType.DMA
    return pl.pallas_call(
        kernel,
        out_shape=(out, out, out),
        in_specs=[
            pl.BlockSpec(memory_space=pl.ANY),
            pl.BlockSpec(memory_space=pl.ANY),
            pl.BlockSpec(memory_space=pltpu.VMEM),
            pl.BlockSpec(memory_space=pltpu.SMEM),
        ],
        out_specs=(pl.BlockSpec(memory_space=pl.ANY),) * 3,
        scratch_shapes=[
            pltpu.VMEM((T, D), F32),
            pltpu.VMEM((T, 2 * G), F32),
            pltpu.VMEM((T, D), BF16),
            pltpu.VMEM((4, T, D), BF16),
            pltpu.VMEM((T, G), F32),
            pltpu.VMEM((5, T, T), BF16),
            pltpu.VMEM((T, G), F32),
            pltpu.VMEM((6, T, G), BF16),
            pltpu.VMEM((6, 4, T, G), BF16),
            pltpu.VMEM((2, T, G), F32),
            pltpu.VMEM((2, T, G), F32),
            pltpu.VMEM((2, T, G), F32),
            pltpu.VMEM((2, T, G), F32),
            pltpu.VMEM((2, 3, T, G), F32),
            pltpu.VMEM((2, 8, G), F32),
            pltpu.VMEM((4, X, 8, G), F32),
            pltpu.VMEM((4, Y, 8, G), F32),
            pltpu.VMEM((4, Z, 8, G), F32),
            dma((2,)),
            dma((2, 3)),
            dma((8,)),
            dma((8,)),
            dma((4,)),
            dma((4,)),
            dma((6, 8)),
            dma((6, 8)),
            dma((4, X + Y + Z - 3)),
            dma((4, X + Y + Z - 3)),
        ],
        compiler_params=pltpu.CompilerParams(
            collective_id=0, has_side_effects=True, vmem_limit_bytes=56 * 2**20
        ),
        name="cascaded_cg",
    )(features, targets, nugget.reshape(1, T), pattern)


def solution(mesh):
    return jax.shard_map(
        body,
        mesh=mesh,
        in_specs=(P("rows", None), P("rows", "out"), P("rows"), P("rows", None)),
        out_specs=(P("rows", "out"), P("rows", "out"), P("rows", "out")),
        check_vma=False,
    )
```

time: 874 us -> 137 us (0.16)
  the two profiles are of different devices: /device:TPU:0 before, /device:TPU:38 now
where the time goes in v1:
time: 137 us
  Pallas kernels  131 us (96%)
  local copies, waits for them, and re-layouts  4.93 us (4%)
    pallas_call x1, Pallas kernels, body(): pl.pallas_call(kernel, out_shape=(out, out, out), in_specs=[pl.BlockSpec(...  131 us
    unnamed x7, local copies, waits for them, and re-layouts  4.93 us

profile of v1, /device:TPU:38, one launch (start us, length us, event | category | flops | bytes accessed | tf_op | source)
XLA Modules:
  0.0 136.8 jit_solution(8901119761834724720)
XLA Ops:
  0.6 131.2 %cascaded_cg.1 = (f32[1024,256]{1,0:T(8,128)}, f32[1024,256]{1,0:T(8,128)}, f32[1024,256]{1,0:T(8,128)}) custom-call(f32[1024,256]{1,0:T(8,128)} %f_hbm.1, f32[1024,256]{1,0:T(8,128)} %t_hbm.1, f32[1,1024]{1,0:T(1,128)} %bitcast.1, s32[1,5]{1,0:T(1,128)} %pat_ref.1), custom_call_target="tpu_custom_call" | custom-call | tf_op jit(solution)/shard_map/cascaded_cg/pallas_call | solution.py:351
  131.9 0.0 copy-start.1
  131.9 2.4 %copy.10 = f32[1024,256]{1,0:T(8,128)} copy(f32[1024,256]{1,0:T(8,128)} %get-tuple-element.6) | data formatting | bytes 2097152
  134.2 0.0 copy-done.1
  134.2 0.0 copy-start
  134.2 1.0 copy.11
  135.2 0.6 copy-done
  135.8 1.0 copy.12
Async XLA Ops:
  131.9 2.4 %copy-start.1 = (f32[1024,256]{1,0:T(8,128)S(1)}, f32[1024,256]{1,0:T(8,128)}, u32[]{:S(2)}) copy-start(f32[1024,256]{1,0:T(8,128)} %get-tuple-element.7) | copy-start | bytes 3145732
  134.2 1.6 %copy-start = (f32[1024,256]{1,0:T(8,128)S(1)}, f32[1024,256]{1,0:T(8,128)}, u32[]{:S(2)}) copy-start(f32[1024,256]{1,0:T(8,128)} %get-tuple-element.8) | copy-start | bytes 3145732

commit v2 on v1

v2 whole, which is shorter than its diff:
```python
import functools
import math

import jax
import jax.numpy as jnp
from jax import lax
from jax.experimental import pallas as pl
from jax.experimental.pallas import tpu as pltpu
from jax.sharding import PartitionSpec as P

MESH = pl.DeviceIdType.MESH
F32, BF16 = jnp.float32, jnp.bfloat16
NT = (((1,), (1,)), ((), ()))
X, Y, Z = 4, 4, 8
NB = X * Y * Z
T = 1024
D = 256
G = 128
H = T // 2
RADIUS = 1.25 * math.sqrt(2.0 * D) / math.sqrt(2.0)
M1, OWN, P1, M2, P2 = range(5)
TILE_OF = (1, 2, 3, 0, 4)
UP, DOWN = 5, 6
COPIES = (
    (OWN, 1, 1, M1),
    (OWN, 0, -1, P1),
    (OWN, 0, 1, M1),
    (OWN, 1, -1, P1),
    (M1, 1, 1, M2),
    (P1, 0, -1, P2),
    (P2, 0, X, M2),
    (M2, 1, -X, P2),
    (OWN, 0, "y+", UP),
    (OWN, 1, "y-", DOWN),
    (UP, 0, "y- +1", M1),
    (DOWN, 1, "y+ -1", P1),
)
SEMS = (0, 1, 2, 3, 4, 5, 6, 7, 8, 9, 2, 3)


def kernel(
    f_hbm, t_hbm, n_ref, pat_ref, sol_hbm, res_hbm, img_hbm,
    f32, t32, f_low, fn, f_relay, na, ktile, diag, nb, e_relay, cur, w1s, w2s, r1s, obuf, coef, xb, yb, zb,
    in_sem, out_sem, f_send, f_recv, sib_send, sib_recv, e_send, e_recv, ar_send, ar_recv,
):
    r, c = lax.axis_index("rows"), lax.axis_index("out")
    x, y, z = lax.rem(r, X), lax.rem(r // X, Y), r // (X * Y)

    def at(step):
        return (lax.rem(r + step + NB, NB), c)

    def along(axis, d):
        if axis == 0:
            return ((z * Y + y) * X + lax.rem(x + d, X), c)
        if axis == 1:
            return ((z * Y + lax.rem(y + d, Y)) * X + x, c)
        return ((lax.rem(z + d, Z) * Y + y) * X + x, c)

    def target(to):
        if isinstance(to, int):
            return at(to)
        if len(to) == 2:
            return along(1, 1 if to == "y+" else Y - 1)
        up = to == "y- +1"
        row, _ = along(1, Y - 1 if up else 1)
        return (lax.rem(row + (1 if up else NB - 1), NB), c)

    sibling = (r, 1 - c)
    load_f = pltpu.make_async_copy(f_hbm, f32, in_sem.at[0])
    load_t = pltpu.make_async_copy(t_hbm, t32, in_sem.at[1])
    load_f.start()
    load_t.start()

    barrier = pltpu.get_barrier_semaphore()
    peers = [at(1), at(-1), at(X), at(-X), at(X * Y - X + 1), at(X - X * Y - 1), sibling]
    for axis, size in enumerate((X, Y, Z)):
        peers += [along(axis, d) for d in range(1, size)]
    for peer in peers:
        pl.semaphore_signal(barrier, inc=1, device_id=peer, device_id_type=MESH)

    def feature_rows(half):
        return pl.ds(pl.multiple_of(c * H + half * (H // 2), H // 2), H // 2)

    def f_copy(i):
        src, half, to, dst = COPIES[i]
        rows = feature_rows(half)

        def ref(slot):
            return f_relay.at[slot - UP] if slot >= UP else fn.at[slot, rows]

        return pltpu.make_async_remote_copy(
            src_ref=ref(src), dst_ref=ref(dst),
            send_sem=f_send.at[SEMS[i]], recv_sem=f_recv.at[SEMS[i]],
            device_id=target(to), device_id_type=MESH,
        )

    def s_copy(slot):
        rows = pl.ds(pl.multiple_of(c * H, H), H)
        return pltpu.make_async_remote_copy(
            src_ref=fn.at[slot, rows], dst_ref=fn.at[slot, rows],
            send_sem=sib_send.at[slot], recv_sem=sib_recv.at[slot],
            device_id=sibling, device_id_type=MESH,
        )

    def e_copy(s, i):
        src, half, to, dst = COPIES[i]
        rows = pl.ds(half * H, H)

        def ref(slot):
            return e_relay.at[s, slot - UP] if slot >= UP else nb.at[s, slot, rows]

        return pltpu.make_async_remote_copy(
            src_ref=ref(src), dst_ref=ref(dst),
            send_sem=e_send.at[s, SEMS[i]], recv_sem=e_recv.at[s, SEMS[i]],
            device_id=target(to), device_id_type=MESH,
        )

    def send(copy):
        copy(0).start()
        copy(1).start()

        @pl.when(x == X - 1)
        def _():
            copy(8).start()

        @pl.when(x < X - 1)
        def _():
            copy(2).start()

        @pl.when(x == 0)
        def _():
            copy(9).start()

        @pl.when(x > 0)
        def _():
            copy(3).start()

    def forward(copy):
        copy(0).wait_recv()
        copy(4).start()
        copy(1).wait_recv()
        copy(5).start()

        @pl.when(x == X - 1)
        def _():
            copy(8).wait_recv()
            copy(10).start()

        @pl.when(x == 0)
        def _():
            copy(9).wait_recv()
            copy(11).start()

    def swap(copy):
        copy(4).wait_recv()
        copy(7).start()
        copy(5).wait_recv()
        copy(6).start()

    def drain(copy):
        for i in range(8):
            copy(i).wait_send()

        @pl.when(x == X - 1)
        def _():
            copy(8).wait_send()

        @pl.when(x == 0)
        def _():
            copy(9).wait_send()

    def exchange(s):
        return functools.partial(e_copy, s)

    def ar_buf(axis, k):
        return ((xb, x), (yb, y), (zb, z))[axis]

    def ar_copies(k, axis):
        buf, own = ar_buf(axis, k)
        first = (0, X - 1, X + Y - 2)[axis]
        return [
            pltpu.make_async_remote_copy(
                src_ref=buf.at[k, own], dst_ref=buf.at[k, own],
                send_sem=ar_send.at[k, first + d - 1], recv_sem=ar_recv.at[k, first + d - 1],
                device_id=along(axis, d), device_id_type=MESH,
            )
            for d in range(1, (X, Y, Z)[axis])
        ]

    def ar_start(k, axis, value):
        buf, own = ar_buf(axis, k)
        buf[k, own] = value
        for copy in ar_copies(k, axis):
            copy.start()

    def ar_finish(k, axis):
        for copy in ar_copies(k, axis):
            copy.wait_recv()
        buf, _ = ar_buf(axis, k)
        total = buf[k, 0]
        for i in range(1, (X, Y, Z)[axis]):
            total = total + buf[k, i]
        return total

    load_f.wait()
    fn[OWN] = f32[...].astype(BF16)
    pl.semaphore_wait(barrier, len(peers))
    send(f_copy)
    f_low[...] = (f32[...] - fn[OWN].astype(F32)).astype(BF16)
    load_t.wait()
    for g in range(2):
        nb[g, OWN] = t32[:, g * G:(g + 1) * G].astype(BF16)
        cur[g] = t32[:, g * G:(g + 1) * G]

    def squares(block, parts):
        wide = block.astype(F32)
        rest = wide * wide
        found = []
        for _ in range(parts):
            found.append(rest.astype(BF16))
            rest = rest - found[-1].astype(F32)
        return found

    def dot_nt(a, b):
        return lax.dot_general(a, b, NT, preferred_element_type=F32)

    halves_col = jnp.full((D, G), 0.5, BF16)
    halves_row = jnp.full((16, D), 0.5, BF16)
    own_squares = squares(f32[...], 3)
    na[...] = sum(jnp.dot(part, halves_col, preferred_element_type=F32) for part in own_squares)
    diag[...] = jnp.zeros_like(diag)

    def build(slot):
        own = slot == OWN
        other = fn[slot]
        parts = own_squares if own else squares(other, 2)
        norms = sum(dot_nt(halves_row, part) for part in parts)
        kept = pat_ref[0, TILE_OF[slot]].astype(F32)
        base = kept * (1.0 / (RADIUS**4 * T))
        slope = kept * (4.0 / (RADIUS**5 * T))
        split = jnp.concatenate([fn[OWN], f_low[...]], axis=1)
        cross = dot_nt(split, jnp.concatenate([other, other], axis=1))
        if own:
            cross = cross + dot_nt(split, jnp.concatenate([f_low[...], f_low[...]], axis=1))
        norm = na[...]
        summed = diag[...]
        for lane in range(T // G):
            cols = slice(lane * G, (lane + 1) * G)
            half_sq = jnp.maximum(norm + norms[0:1, cols] - cross[:, cols], 1e-30)
            dist = half_sq * lax.rsqrt(half_sq)
            fall = jnp.maximum(RADIUS - dist, 0.0)
            fall = fall * fall
            value = (fall * fall) * (dist * slope + base)
            start = slot * T + lane * G
            ktile[:, start:start + G] = value.astype(BF16)
            summed = summed + value
        diag[...] = summed

    build(OWN)
    forward(f_copy)
    send(exchange(0))
    f_copy(2).wait_recv()
    s_copy(M1).start()
    f_copy(3).wait_recv()
    s_copy(P1).start()
    s_copy(M1).wait_recv()
    build(M1)
    swap(f_copy)
    s_copy(P1).wait_recv()
    build(P1)
    forward(exchange(0))
    send(exchange(1))
    f_copy(6).wait_recv()
    s_copy(M2).start()
    f_copy(7).wait_recv()
    s_copy(P2).start()
    s_copy(M2).wait_recv()
    build(M2)
    swap(exchange(0))
    s_copy(P2).wait_recv()
    build(P2)
    nugget = jnp.broadcast_to(n_ref[0:1, :], (G, T)).T
    diag[...] = nugget + jnp.sum(diag[...], axis=1, keepdims=True)

    def out_copy(g, i):
        cols = pl.ds(pl.multiple_of(g * G, G), G)
        out = (sol_hbm, res_hbm, img_hbm)[i]
        return pltpu.make_async_copy(obuf.at[g, i], out.at[:, cols], out_sem.at[g, i])

    def step(s, _):
        g, e = lax.rem(s, 2), s // 2
        cols = pl.ds(pl.multiple_of(g * G, G), G)

        def product(first, last):
            return jnp.dot(
                ktile[:, first * T:(last + 1) * T],
                nb[s, first:last + 1].reshape((last + 1 - first) * T, G),
                preferred_element_type=F32,
            )

        e_copy(s, 2).wait_recv()
        e_copy(s, 3).wait_recv()
        w2s[g] = diag[...] * cur[g] + product(M1, P1)

        @pl.when(s >= 1)
        def _():
            swap(exchange(s))

        @pl.when(s <= 4)
        def _():
            forward(exchange(s + 1))

        @pl.when((s >= 1) & (s <= 4))
        def _():
            ar_start(s - 1, 1, ar_finish(s - 1, 0))

        @pl.when(e == 2)
        def _():
            total = ar_finish(s - 2, 2)
            norm, cross = total[0:1, :], total[1:2, :]
            step0 = coef[g, 1:2, :]
            momentum = norm / coef[g, 0:1, :]
            step1 = norm / (cross - momentum * norm / step0)
            coef[g, 2:3, :] = momentum
            coef[g, 3:4, :] = step1
            start = t32[:, cols]
            res = r1s[g]
            obuf[g, 0] = step0 * start + step1 * (res + momentum * start)
            obuf[g, 1] = res - step1 * (cur[g] + momentum * w1s[g])
            out_copy(g, 0).start()
            out_copy(g, 1).start()

        e_copy(s, 6).wait_recv()
        e_copy(s, 7).wait_recv()
        w2s[g] = w2s[g] + product(M2, P2)

        def reduce_start(norm, cross):
            ar_start(s, 0, jnp.concatenate(
                [jnp.sum(norm, axis=0, keepdims=True), jnp.sum(cross, axis=0, keepdims=True),
                 jnp.zeros((6, G), F32)], axis=0))

        @pl.when(e == 0)
        def _():
            w = w2s[g]
            nb[s + 2, OWN] = w.astype(BF16)
            send(exchange(s + 2))
            start = t32[:, cols]
            cur[g] = w
            w1s[g] = w
            reduce_start(start * start, w * start)

        @pl.when(e == 1)
        def _():
            total = ar_finish(s - 2, 2)
            norm, cross = total[0:1, :], total[1:2, :]
            step0 = norm / cross
            coef[g, 0:1, :] = norm
            coef[g, 1:2, :] = step0
            image = cur[g] - step0 * w2s[g]
            nb[s + 2, OWN] = image.astype(BF16)
            send(exchange(s + 2))
            cur[g] = image
            res = t32[:, cols] - step0 * w1s[g]
            r1s[g] = res
            obuf[g, 2] = w2s[g]
            reduce_start(res * res, image * res)

        @pl.when(e == 2)
        def _():
            momentum, step1 = coef[g, 2:3, :], coef[g, 3:4, :]
            obuf[g, 2] = cur[g] - step1 * (w2s[g] + momentum * obuf[g, 2])
            out_copy(g, 2).start()

        @pl.when((s >= 1) & (s <= 4))
        def _():
            ar_start(s - 1, 2, ar_finish(s - 1, 1))

        return 0

    lax.fori_loop(0, 6, step, 0)

    drain(f_copy)
    for slot in (M1, P1, M2, P2):
        s_copy(slot).wait_send()

    def finish(s, _):
        drain(exchange(s))

        @pl.when(s < 4)
        def _():
            for axis in range(3):
                for copy in ar_copies(s, axis):
                    copy.wait_send()

        @pl.when(s < 2)
        def _():
            for i in range(3):
                out_copy(s, i).wait()

        return 0

    lax.fori_loop(0, 6, finish, 0)


def body(features, targets, nugget, pattern):
    out = jax.ShapeDtypeStruct((T, 2 * G), F32)
    dma = pltpu.SemaphoreType.DMA
    return pl.pallas_call(
        kernel,
        out_shape=(out, out, out),
        in_specs=[
            pl.BlockSpec(memory_space=pl.ANY),
            pl.BlockSpec(memory_space=pl.ANY),
            pl.BlockSpec(memory_space=pltpu.VMEM),
            pl.BlockSpec(memory_space=pltpu.SMEM),
        ],
        out_specs=(pl.BlockSpec(memory_space=pl.ANY),) * 3,
        scratch_shapes=[
            pltpu.VMEM((T, D), F32),
            pltpu.VMEM((T, 2 * G), F32),
            pltpu.VMEM((T, D), BF16),
            pltpu.VMEM((5, T, D), BF16),
            pltpu.VMEM((2, H // 2, D), BF16),
            pltpu.VMEM((T, G), F32),
            pltpu.VMEM((T, 5 * T), BF16),
            pltpu.VMEM((T, G), F32),
            pltpu.VMEM((6, 5, T, G), BF16),
            pltpu.VMEM((6, 2, H, G), BF16),
            pltpu.VMEM((2, T, G), F32),
            pltpu.VMEM((2, T, G), F32),
            pltpu.VMEM((2, T, G), F32),
            pltpu.VMEM((2, T, G), F32),
            pltpu.VMEM((2, 3, T, G), F32),
            pltpu.VMEM((2, 8, G), F32),
            pltpu.VMEM((4, X, 8, G), F32),
            pltpu.VMEM((4, Y, 8, G), F32),
            pltpu.VMEM((4, Z, 8, G), F32),
            dma((2,)),
            dma((2, 3)),
            dma((10,)),
            dma((10,)),
            dma((5,)),
            dma((5,)),
            dma((6, 10)),
            dma((6, 10)),
            dma((4, X + Y + Z - 3)),
            dma((4, X + Y + Z - 3)),
        ],
        compiler_params=pltpu.CompilerParams(
            collective_id=0, has_side_effects=True, vmem_limit_bytes=56 * 2**20
        ),
        name="cascaded_cg",
    )(features, targets, nugget.reshape(1, T), pattern)


def solution(mesh):
    return jax.shard_map(
        body,
        mesh=mesh,
        in_specs=(P("rows", None), P("rows", "out"), P("rows"), P("rows", None)),
        out_specs=(P("rows", "out"), P("rows", "out"), P("rows", "out")),
        check_vma=False,
    )
```

time: 137 us -> 135 us (0.985)
  the two profiles are of different devices: /device:TPU:38 before, /device:TPU:2 now
where the time goes in v2:
time: 135 us
  Pallas kernels  129 us (96%)
  local copies, waits for them, and re-layouts  4.93 us (4%)
    pallas_call x1, Pallas kernels, body(): pl.pallas_call(kernel, out_shape=(out, out, out), in_specs=[pl.BlockSpec(...  129 us
    unnamed x7, local copies, waits for them, and re-layouts  4.93 us

profile of v2, /device:TPU:2, one launch (start us, length us, event | category | flops | bytes accessed | tf_op | source)
XLA Modules:
  0.0 134.7 jit_solution(4351410097818784968)
XLA Ops:
  0.6 129.1 %cascaded_cg.1 = (f32[1024,256]{1,0:T(8,128)}, f32[1024,256]{1,0:T(8,128)}, f32[1024,256]{1,0:T(8,128)}) custom-call(f32[1024,256]{1,0:T(8,128)} %f_hbm.1, f32[1024,256]{1,0:T(8,128)} %t_hbm.1, f32[1,1024]{1,0:T(1,128)} %bitcast.1, s32[1,5]{1,0:T(1,128)} %pat_ref.1), custom_call_target="tpu_custom_call" | custom-call | tf_op jit(solution)/shard_map/cascaded_cg/pallas_call | solution.py:408
  129.8 0.0 copy-start.1
  129.8 2.4 %copy.10 = f32[1024,256]{1,0:T(8,128)} copy(f32[1024,256]{1,0:T(8,128)} %get-tuple-element.6) | data formatting | bytes 2097152
  132.1 0.0 copy-done.1
  132.1 0.0 copy-start
  132.1 1.0 copy.11
  133.1 0.6 copy-done
  133.7 1.0 copy.12
Async XLA Ops:
  129.8 2.4 %copy-start.1 = (f32[1024,256]{1,0:T(8,128)S(1)}, f32[1024,256]{1,0:T(8,128)}, u32[]{:S(2)}) copy-start(f32[1024,256]{1,0:T(8,128)} %get-tuple-element.7) | copy-start | bytes 3145732
  132.1 1.6 %copy-start = (f32[1024,256]{1,0:T(8,128)S(1)}, f32[1024,256]{1,0:T(8,128)}, u32[]{:S(2)}) copy-start(f32[1024,256]{1,0:T(8,128)} %get-tuple-element.8) | copy-start | bytes 3145732

commit v3 on v2

--- a/solution.py
+++ b/solution.py
@@ -21,6 +21,11 @@
 M1, OWN, P1, M2, P2 = range(5)
 TILE_OF = (1, 2, 3, 0, 4)
 UP, DOWN = 5, 6
+PLACE = {
+    (M1, 1): 0, (OWN, 0): 1, (OWN, 1): 2, (P1, 0): 3,
+    (M1, 0): 4, (M2, 1): 5, (P2, 0): 6, (P1, 1): 7,
+    (M2, 0): 8, (P2, 1): 9,
+}
 COPIES = (
     (OWN, 1, 1, M1),
     (OWN, 0, -1, P1),
@@ -40,7 +45,7 @@
 
 def kernel(
     f_hbm, t_hbm, n_ref, pat_ref, sol_hbm, res_hbm, img_hbm,
-    f32, t32, f_low, fn, f_relay, na, ktile, diag, nb, e_relay, cur, w1s, w2s, r1s, obuf, coef, xb, yb, zb,
+    f32, t32, f_low, fn, na, ktile, diag, nb, e_relay, cur, w1s, w2s, r1s, obuf, coef, xb, yb, zb,
     in_sem, out_sem, f_send, f_recv, sib_send, sib_recv, e_send, e_recv, ar_send, ar_recv,
 ):
     r, c = lax.axis_index("rows"), lax.axis_index("out")
@@ -85,12 +90,9 @@
         src, half, to, dst = COPIES[i]
         rows = feature_rows(half)
 
-        def ref(slot):
-            return f_relay.at[slot - UP] if slot >= UP else fn.at[slot, rows]
-
         return pltpu.make_async_remote_copy(
-            src_ref=ref(src), dst_ref=ref(dst),
-            send_sem=f_send.at[SEMS[i]], recv_sem=f_recv.at[SEMS[i]],
+            src_ref=fn.at[src, rows], dst_ref=fn.at[dst, rows],
+            send_sem=f_send.at[i], recv_sem=f_recv.at[i],
             device_id=target(to), device_id_type=MESH,
         )
 
@@ -104,10 +106,9 @@
 
     def e_copy(s, i):
         src, half, to, dst = COPIES[i]
-        rows = pl.ds(half * H, H)
 
         def ref(slot):
-            return e_relay.at[s, slot - UP] if slot >= UP else nb.at[s, slot, rows]
+            return e_relay.at[s, slot - UP] if slot >= UP else nb.at[s, PLACE[slot, half]]
 
         return pltpu.make_async_remote_copy(
             src_ref=ref(src), dst_ref=ref(dst),
@@ -115,6 +116,10 @@
             device_id=target(to), device_id_type=MESH,
         )
 
+    def put(s, field):
+        for half in range(2):
+            nb[s, PLACE[OWN, half]] = field[half * H:(half + 1) * H].astype(BF16)
+
     def send(copy):
         copy(0).start()
         copy(1).start()
@@ -135,11 +140,13 @@
         def _():
             copy(3).start()
 
-    def forward(copy):
+    def forward(copy, relayed=True):
         copy(0).wait_recv()
         copy(4).start()
         copy(1).wait_recv()
         copy(5).start()
+        if not relayed:
+            return
 
         @pl.when(x == X - 1)
         def _():
@@ -205,11 +212,12 @@
     load_f.wait()
     fn[OWN] = f32[...].astype(BF16)
     pl.semaphore_wait(barrier, len(peers))
-    send(f_copy)
+    for i in range(4):
+        f_copy(i).start()
     f_low[...] = (f32[...] - fn[OWN].astype(F32)).astype(BF16)
     load_t.wait()
     for g in range(2):
-        nb[g, OWN] = t32[:, g * G:(g + 1) * G].astype(BF16)
+        put(g, t32[:, g * G:(g + 1) * G])
         cur[g] = t32[:, g * G:(g + 1) * G]
 
     def squares(block, parts):
@@ -251,13 +259,13 @@
             fall = jnp.maximum(RADIUS - dist, 0.0)
             fall = fall * fall
             value = (fall * fall) * (dist * slope + base)
-            start = slot * T + lane * G
+            start = PLACE[slot, lane * G // H] * H + lane * G % H
             ktile[:, start:start + G] = value.astype(BF16)
             summed = summed + value
         diag[...] = summed
 
     build(OWN)
-    forward(f_copy)
+    forward(f_copy, relayed=False)
     send(exchange(0))
     f_copy(2).wait_recv()
     s_copy(M1).start()
@@ -293,22 +301,24 @@
 
         def product(first, last):
             return jnp.dot(
-                ktile[:, first * T:(last + 1) * T],
-                nb[s, first:last + 1].reshape((last + 1 - first) * T, G),
+                ktile[:, first * H:last * H],
+                nb[s, first:last].reshape((last - first) * H, G),
                 preferred_element_type=F32,
             )
 
+        w2s[g] = diag[...] * cur[g] + product(0, 4)
+
+        @pl.when(s >= 1)
+        def _():
+            swap(exchange(s))
+
+        @pl.when(s <= 4)
+        def _():
+            forward(exchange(s + 1))
+
         e_copy(s, 2).wait_recv()
         e_copy(s, 3).wait_recv()
-        w2s[g] = diag[...] * cur[g] + product(M1, P1)
-
-        @pl.when(s >= 1)
-        def _():
-            swap(exchange(s))
-
-        @pl.when(s <= 4)
-        def _():
-            forward(exchange(s + 1))
+        w2s[g] = w2s[g] + product(4, 8)
 
         @pl.when((s >= 1) & (s <= 4))
         def _():
@@ -332,7 +342,7 @@
 
         e_copy(s, 6).wait_recv()
         e_copy(s, 7).wait_recv()
-        w2s[g] = w2s[g] + product(M2, P2)
+        w2s[g] = w2s[g] + product(8, 10)
 
         def reduce_start(norm, cross):
             ar_start(s, 0, jnp.concatenate(
@@ -342,7 +352,7 @@
         @pl.when(e == 0)
         def _():
             w = w2s[g]
-            nb[s + 2, OWN] = w.astype(BF16)
+            put(s + 2, w)
             send(exchange(s + 2))
             start = t32[:, cols]
             cur[g] = w
@@ -357,7 +367,7 @@
             coef[g, 0:1, :] = norm
             coef[g, 1:2, :] = step0
             image = cur[g] - step0 * w2s[g]
-            nb[s + 2, OWN] = image.astype(BF16)
+            put(s + 2, image)
             send(exchange(s + 2))
             cur[g] = image
             res = t32[:, cols] - step0 * w1s[g]
@@ -379,7 +389,8 @@
 
     lax.fori_loop(0, 6, step, 0)
 
-    drain(f_copy)
+    for i in range(8):
+        f_copy(i).wait_send()
     for slot in (M1, P1, M2, P2):
         s_copy(slot).wait_send()
 
@@ -404,6 +415,7 @@
 
 def body(features, targets, nugget, pattern):
     out = jax.ShapeDtypeStruct((T, 2 * G), F32)
+    inputs = (features, targets, nugget.reshape(1, T), pattern)
     dma = pltpu.SemaphoreType.DMA
     return pl.pallas_call(
         kernel,
@@ -420,11 +432,10 @@
             pltpu.VMEM((T, 2 * G), F32),
             pltpu.VMEM((T, D), BF16),
             pltpu.VMEM((5, T, D), BF16),
-            pltpu.VMEM((2, H // 2, D), BF16),
             pltpu.VMEM((T, G), F32),
             pltpu.VMEM((T, 5 * T), BF16),
             pltpu.VMEM((T, G), F32),
-            pltpu.VMEM((6, 5, T, G), BF16),
+            pltpu.VMEM((6, 10, H, G), BF16),
             pltpu.VMEM((6, 2, H, G), BF16),
             pltpu.VMEM((2, T, G), F32),
             pltpu.VMEM((2, T, G), F32),
@@ -437,8 +448,8 @@
             pltpu.VMEM((4, Z, 8, G), F32),
             dma((2,)),
             dma((2, 3)),
-            dma((10,)),
-            dma((10,)),
+            dma((8,)),
+            dma((8,)),
             dma((5,)),
             dma((5,)),
             dma((6, 10)),
@@ -447,10 +458,10 @@
             dma((4, X + Y + Z - 3)),
         ],
         compiler_params=pltpu.CompilerParams(
-            collective_id=0, has_side_effects=True, vmem_limit_bytes=56 * 2**20
+            collective_id=0, has_side_effects=True, vmem_limit_bytes=46 * 2**20
         ),
         name="cascaded_cg",
-    )(features, targets, nugget.reshape(1, T), pattern)
+    )(*(pltpu.with_memory_space_constraint(array, pltpu.HBM) for array in inputs))
 
 
 def solution(mesh):

time: 135 us -> 108 us (0.80)
  the two profiles are of different devices: /device:TPU:2 before, /device:TPU:0 now
where the time goes in v3:
time: 108 us
  Pallas kernels  105 us (97%)
  local copies, waits for them, and re-layouts  2.91 us (3%)
    pallas_call x1, Pallas kernels, body(): pl.pallas_call(kernel, out_shape=(out, out, out), in_specs=[pl.BlockSpec(...  105 us
    unnamed x3, local copies, waits for them, and re-layouts  2.91 us

profile of v3, /device:TPU:0, one launch (start us, length us, event | category | flops | bytes accessed | tf_op | source)
XLA Modules:
  0.0 108.1 jit_solution(10535696140953926976)
XLA Ops:
  0.6 104.5 %cascaded_cg.1 = (f32[1024,256]{1,0:T(8,128)S(1)}, f32[1024,256]{1,0:T(8,128)S(1)}, f32[1024,256]{1,0:T(8,128)S(1)}) custom-call(f32[1024,256]{1,0:T(8,128)} %f_hbm.1, f32[1024,256]{1,0:T(8,128)} %t_hbm.1, f32[1,1024]{1,0:T(1,128)} %bitcast.1, s32[1,5]{1,0:T(1,128)} %pat_ref.1), custom_call_target="tpu_custom_call" | custom-call | tf_op jit(solution)/shard_map/cascaded_cg/pallas_call | solution.py:420
  105.2 1.0 copy.10
  106.1 1.0 copy.11
  107.1 1.0 copy.12

commit v4 on v3

--- a/solution.py
+++ b/solution.py
@@ -44,9 +44,9 @@
 
 
 def kernel(
-    f_hbm, t_hbm, n_ref, pat_ref, sol_hbm, res_hbm, img_hbm,
-    f32, t32, f_low, fn, na, ktile, diag, nb, e_relay, cur, w1s, w2s, r1s, obuf, coef, xb, yb, zb,
-    in_sem, out_sem, f_send, f_recv, sib_send, sib_recv, e_send, e_recv, ar_send, ar_recv,
+    f_hbm, t_hbm, n_ref, pat_ref, sol_ref, res_ref, img_ref,
+    f32, t32, f_low, fn, na, ktile, diag, nb, e_relay, cur, w1s, w2s, r1s, steps, coef, xb, yb, zb,
+    in_sem, f_send, f_recv, sib_send, sib_recv, e_send, e_recv, ar_send, ar_recv,
 ):
     r, c = lax.axis_index("rows"), lax.axis_index("out")
     x, y, z = lax.rem(r, X), lax.rem(r // X, Y), r // (X * Y)
@@ -290,11 +290,6 @@
     nugget = jnp.broadcast_to(n_ref[0:1, :], (G, T)).T
     diag[...] = nugget + jnp.sum(diag[...], axis=1, keepdims=True)
 
-    def out_copy(g, i):
-        cols = pl.ds(pl.multiple_of(g * G, G), G)
-        out = (sol_hbm, res_hbm, img_hbm)[i]
-        return pltpu.make_async_copy(obuf.at[g, i], out.at[:, cols], out_sem.at[g, i])
-
     def step(s, _):
         g, e = lax.rem(s, 2), s // 2
         cols = pl.ds(pl.multiple_of(g * G, G), G)
@@ -322,11 +317,11 @@
 
         @pl.when((s >= 1) & (s <= 4))
         def _():
-            ar_start(s - 1, 1, ar_finish(s - 1, 0))
+            ar_start(s - 1, 1, ar_finish(s - 1, 2))
 
         @pl.when(e == 2)
         def _():
-            total = ar_finish(s - 2, 2)
+            total = ar_finish(s - 2, 0)
             norm, cross = total[0:1, :], total[1:2, :]
             step0 = coef[g, 1:2, :]
             momentum = norm / coef[g, 0:1, :]
@@ -335,17 +330,15 @@
             coef[g, 3:4, :] = step1
             start = t32[:, cols]
             res = r1s[g]
-            obuf[g, 0] = step0 * start + step1 * (res + momentum * start)
-            obuf[g, 1] = res - step1 * (cur[g] + momentum * w1s[g])
-            out_copy(g, 0).start()
-            out_copy(g, 1).start()
+            sol_ref[:, cols] = step0 * start + step1 * (res + momentum * start)
+            res_ref[:, cols] = res - step1 * (cur[g] + momentum * w1s[g])
 
         e_copy(s, 6).wait_recv()
         e_copy(s, 7).wait_recv()
         w2s[g] = w2s[g] + product(8, 10)
 
         def reduce_start(norm, cross):
-            ar_start(s, 0, jnp.concatenate(
+            ar_start(s, 2, jnp.concatenate(
                 [jnp.sum(norm, axis=0, keepdims=True), jnp.sum(cross, axis=0, keepdims=True),
                  jnp.zeros((6, G), F32)], axis=0))
 
@@ -361,7 +354,7 @@
 
         @pl.when(e == 1)
         def _():
-            total = ar_finish(s - 2, 2)
+            total = ar_finish(s - 2, 0)
             norm, cross = total[0:1, :], total[1:2, :]
             step0 = norm / cross
             coef[g, 0:1, :] = norm
@@ -372,18 +365,17 @@
             cur[g] = image
             res = t32[:, cols] - step0 * w1s[g]
             r1s[g] = res
-            obuf[g, 2] = w2s[g]
+            steps[g] = w2s[g]
             reduce_start(res * res, image * res)
 
         @pl.when(e == 2)
         def _():
             momentum, step1 = coef[g, 2:3, :], coef[g, 3:4, :]
-            obuf[g, 2] = cur[g] - step1 * (w2s[g] + momentum * obuf[g, 2])
-            out_copy(g, 2).start()
+            img_ref[:, cols] = cur[g] - step1 * (w2s[g] + momentum * steps[g])
 
         @pl.when((s >= 1) & (s <= 4))
         def _():
-            ar_start(s - 1, 2, ar_finish(s - 1, 1))
+            ar_start(s - 1, 0, ar_finish(s - 1, 1))
 
         return 0
 
@@ -402,11 +394,6 @@
             for axis in range(3):
                 for copy in ar_copies(s, axis):
                     copy.wait_send()
-
-        @pl.when(s < 2)
-        def _():
-            for i in range(3):
-                out_copy(s, i).wait()
 
         return 0
 
@@ -426,7 +413,7 @@
             pl.BlockSpec(memory_space=pltpu.VMEM),
             pl.BlockSpec(memory_space=pltpu.SMEM),
         ],
-        out_specs=(pl.BlockSpec(memory_space=pl.ANY),) * 3,
+        out_specs=(pl.BlockSpec(memory_space=pltpu.VMEM),) * 3,
         scratch_shapes=[
             pltpu.VMEM((T, D), F32),
             pltpu.VMEM((T, 2 * G), F32),
@@ -441,13 +428,12 @@
             pltpu.VMEM((2, T, G), F32),
             pltpu.VMEM((2, T, G), F32),
             pltpu.VMEM((2, T, G), F32),
-            pltpu.VMEM((2, 3, T, G), F32),
+            pltpu.VMEM((2, T, G), F32),
             pltpu.VMEM((2, 8, G), F32),
             pltpu.VMEM((4, X, 8, G), F32),
             pltpu.VMEM((4, Y, 8, G), F32),
             pltpu.VMEM((4, Z, 8, G), F32),
             dma((2,)),
-            dma((2, 3)),
             dma((8,)),
             dma((8,)),
             dma((5,)),

time: 108 us -> 108 us (level)
  no operation moved by 1% of the time
where the time goes in v4:
time: 108 us
  Pallas kernels  104 us (96%)
  local copies, waits for them, and re-layouts  2.91 us (3%)
    pallas_call x1, Pallas kernels, body(): pl.pallas_call(kernel, out_shape=(out, out, out), in_specs=[pl.BlockSpec(...  104 us
    unnamed x3, local copies, waits for them, and re-layouts  2.91 us

profile of v4, /device:TPU:0, one launch (start us, length us, event | category | flops | bytes accessed | tf_op | source)
XLA Modules:
  0.0 107.9 jit_solution(404829682065214326)
XLA Ops:
  0.6 104.4 %cascaded_cg.1 = (f32[1024,256]{1,0:T(8,128)S(1)}, f32[1024,256]{1,0:T(8,128)S(1)}, f32[1024,256]{1,0:T(8,128)S(1)}) custom-call(f32[1024,256]{1,0:T(8,128)} %f_hbm.1, f32[1024,256]{1,0:T(8,128)} %t_hbm.1, f32[1,1024]{1,0:T(1,128)} %bitcast.1, s32[1,5]{1,0:T(1,128)} %pat_ref.1), custom_call_target="tpu_custom_call" | custom-call | tf_op jit(solution)/shard_map/cascaded_cg/pallas_call | solution.py:407
  105.0 1.0 copy.10
  106.0 1.0 copy.11
  107.0 1.0 copy.12
